TPU v7x, 32 devices: a whole 2x2x4 slice. The times are simulated.
32 devices in a mesh: lat: 4 (over x, core), lon: 4 (over z), ch: 2 (over y).
Axes of the slice: x: 2, y: 2, z: 4, core: 2. Of those that a mesh axis runs over, the one named last changes fastest.
Arguments:
- grid_tokens: bfloat16 [1, 256, 768, 768], P(None, 'lat', 'lon'), may hold values from -6 to 6
- first_gain: float32 [768], replicated, may hold values from 0.1 to 1.9
- first_bias: float32 [768], replicated, may hold values from -3 to 3
- first_filter: bfloat16 [2, 8, 96, 96], P(None, 'ch'), may hold values from -0.4375 to 0.4375
- first_shift: float32 [2, 8, 96], P(None, 'ch'), may hold values from -3 to 3
- second_filter: bfloat16 [2, 8, 96, 96], P(None, 'ch'), may hold values from -0.4375 to 0.4375
- second_shift: float32 [2, 8, 96], P(None, 'ch'), may hold values from -3 to 3
- mode_mask: int32 [256, 384], P(None, ('lat', 'lon')), may hold values 0 or 1
- second_gain: float32 [768], replicated, may hold values from 0.1 to 1.9
- second_bias: float32 [768], replicated, may hold values from -3 to 3
- up_weight: bfloat16 [768, 3072], P(None, 'ch'), may hold values from -0.21875 to 0.21875
- up_bias: float32 [3072], P('ch'), may hold values from -3 to 3
- down_weight: bfloat16 [3072, 768], P('ch'), may hold values from -0.109375 to 0.109375
- down_bias: float32 [768], P('ch'), may hold values from -3 to 3
Outputs:
- block_output: bfloat16 [1, 256, 768, 768], P(None, ('lat', 'lon'), None, 'ch')
Inputs may be any that keep to these rules, and one draw needn't show every extreme that they name: `mode_mask`: 1 keeps a mode, 0 drops it.
All inputs are finite; a program needn't handle non-finite values. No bound on the sum of `mode_mask` on one device may be relied on, other than what follows from the above.
Results may differ from a plain program's by a relative error of at most 0.009.
Values may be sent and summed in bfloat16 or wider, within the bound.
A program may use at most 192 MiB of HBM per device.

v0:
```python
import math

import jax
import jax.numpy as jnp
from jax import lax
from jax.sharding import PartitionSpec as P

shrink_level = 0.01
norm_epsilon = 1e-05


def lon_tables(lon_width, mode_count):
    frequency = jnp.arange(mode_count, dtype=jnp.int32)[:, None]
    position = jnp.arange(lon_width, dtype=jnp.int32)[None, :]
    phases = frequency * position % lon_width
    angles = phases.astype(jnp.float32) * (2.0 * math.pi / lon_width)
    norm_scale = 1.0 / math.sqrt(lon_width)
    forward = jnp.stack([jnp.cos(angles) * norm_scale, -jnp.sin(angles) * norm_scale]).astype(
        jnp.bfloat16
    )
    factor = jnp.where(frequency == 0, 1.0, 2.0) * norm_scale
    inverse = jnp.stack([jnp.cos(angles) * factor, -jnp.sin(angles) * factor]).astype(jnp.bfloat16)
    return (forward, inverse)


def lat_tables(lat_height):
    indices = jnp.arange(lat_height, dtype=jnp.int32)
    phases = indices[:, None] * indices[None, :] % lat_height
    angles = phases.astype(jnp.float32) * (2.0 * math.pi / lat_height)
    norm_scale = 1.0 / math.sqrt(lat_height)
    cosine = jnp.cos(angles) * norm_scale
    sine_table = jnp.sin(angles) * norm_scale
    forward = jnp.stack([jnp.stack([cosine, sine_table]), jnp.stack([-sine_table, cosine])]).astype(
        jnp.bfloat16
    )
    inverse = jnp.stack([jnp.stack([cosine, -sine_table]), jnp.stack([sine_table, cosine])]).astype(
        jnp.bfloat16
    )
    return (forward, inverse)


def complex_weight(weights):
    real_part, imag_part = (weights[0], weights[1])
    top_half = jnp.stack([real_part, imag_part], axis=2)
    low_half = jnp.stack([-imag_part, real_part], axis=2)
    return jnp.stack([top_half, low_half])


def mode_mixer(spectrum, weight_one, shift_one, weight_two, shift_two, keep_mask):
    samples, _, lat_freqs, lon_freqs, channel_count = spectrum.shape
    block_count = weight_one.shape[1]
    block_width = weight_one.shape[2]
    split_spec = spectrum.reshape(samples, 2, lat_freqs, lon_freqs, block_count, block_width)
    first_layer = jnp.einsum(
        "bpxyni,pniqo->bqxyno",
        split_spec,
        complex_weight(weight_one),
        preferred_element_type=jnp.float32,
    )
    first_layer = jnp.maximum(first_layer + shift_one[None, :, None, None, :, :], 0.0).astype(
        jnp.bfloat16
    )
    second_layer = jnp.einsum(
        "bpxyni,pniqo->bqxyno",
        first_layer,
        complex_weight(weight_two),
        preferred_element_type=jnp.float32,
    )
    second_layer = second_layer + shift_two[None, :, None, None, :, :]
    second_layer = second_layer - jnp.clip(second_layer, -shrink_level, shrink_level)
    second_layer = second_layer * keep_mask.astype(jnp.float32)[None, None, :, :, None, None]
    return second_layer.astype(jnp.bfloat16).reshape(
        samples, 2, lat_freqs, lon_freqs, channel_count
    )


def shards(
    grid_tokens,
    first_gain,
    first_bias,
    first_filter,
    first_shift,
    second_filter,
    second_shift,
    mode_mask,
    second_gain,
    second_bias,
    up_weight,
    up_bias,
    down_weight,
    down_bias,
):
    lat_count = lax.axis_size("lat")
    lon_count = lax.axis_size("lon")
    ch_count = lax.axis_size("ch")
    samples, rows_here, cols_here, channel_count = grid_tokens.shape
    full_width = cols_here * lon_count
    full_height = rows_here * lat_count
    part_chans = channel_count // ch_count
    offset = lax.axis_index("ch") * part_chans
    spread_count = lat_count * lon_count
    modes_here = full_width // 2 // spread_count
    values = grid_tokens.astype(jnp.float32)
    center = jnp.mean(values, axis=-1, keepdims=True)
    inv_dev = lax.rsqrt(
        jnp.mean(jnp.square(values - center), axis=-1, keepdims=True) + norm_epsilon
    )
    token_part = lax.dynamic_slice_in_dim(grid_tokens, offset, part_chans, 3)
    gain_part = lax.dynamic_slice_in_dim(first_gain, offset, part_chans, 0)
    bias_part = lax.dynamic_slice_in_dim(first_bias, offset, part_chans, 0)
    token_rows = lax.all_to_all(token_part, "lon", split_axis=1, concat_axis=2, tiled=True)
    moments = lax.all_to_all(
        jnp.concatenate([center, inv_dev], axis=3), "lon", split_axis=1, concat_axis=2, tiled=True
    )
    normed_rows = (
        (token_rows.astype(jnp.float32) - moments[..., 0:1]) * moments[..., 1:2] * gain_part
        + bias_part
    ).astype(jnp.bfloat16)
    row_pairs = normed_rows.shape[1]
    lon_forward, lon_inverse = lon_tables(full_width, full_width // 2)
    lat_forward, lat_inverse = lat_tables(full_height)
    row_spectrum = jnp.einsum(
        "pkw,brwc->brpkc", lon_forward, normed_rows, preferred_element_type=jnp.float32
    ).astype(jnp.bfloat16)
    packed = row_spectrum.reshape(samples, 1, row_pairs, 2, spread_count, modes_here, part_chans)
    arrived = lax.all_to_all(packed, ("lat", "lon"), split_axis=4, concat_axis=1, tiled=True)
    spectrum_rows = arrived.reshape(samples, full_height, 2, modes_here, part_chans)
    spectrum = jnp.einsum(
        "qpxh,bhpyc->bqxyc", lat_forward, spectrum_rows, preferred_element_type=jnp.float32
    ).astype(jnp.bfloat16)
    filtered_modes = mode_mixer(
        spectrum, first_filter, first_shift, second_filter, second_shift, mode_mask
    )
    back_rows = jnp.einsum(
        "qphx,bpxyc->bhqyc", lat_inverse, filtered_modes, preferred_element_type=jnp.float32
    ).astype(jnp.bfloat16)
    packed_back = back_rows.reshape(samples, spread_count, row_pairs, 2, 1, modes_here, part_chans)
    returned = lax.all_to_all(packed_back, ("lat", "lon"), split_axis=1, concat_axis=4, tiled=True)
    row_modes = returned.reshape(samples, row_pairs, 2, full_width // 2, part_chans)
    filtered = jnp.einsum(
        "pkw,brpkc->brwc", lon_inverse, row_modes, preferred_element_type=jnp.float32
    )
    mixed = (token_rows.astype(jnp.float32) + normed_rows.astype(jnp.float32) + filtered).astype(
        jnp.bfloat16
    )
    all_channels = lax.all_gather(mixed, "ch", axis=3, tiled=True).astype(jnp.float32)
    center_two = jnp.mean(all_channels, axis=-1, keepdims=True)
    inv_two = lax.rsqrt(
        jnp.mean(jnp.square(all_channels - center_two), axis=-1, keepdims=True) + norm_epsilon
    )
    normed_two = ((all_channels - center_two) * inv_two * second_gain + second_bias).astype(
        jnp.bfloat16
    )
    tokens = normed_two.reshape(-1, channel_count)
    hidden = jnp.dot(tokens, up_weight, preferred_element_type=jnp.float32) + up_bias
    hidden = jax.nn.gelu(hidden, approximate=False).astype(jnp.bfloat16)
    partial_rows = jnp.dot(hidden, down_weight, preferred_element_type=jnp.float32).reshape(
        samples, row_pairs, full_width, channel_count
    )
    summed = lax.psum_scatter(
        partial_rows.astype(jnp.bfloat16), "ch", scatter_dimension=3, tiled=True
    ).astype(jnp.float32)
    return (mixed.astype(jnp.float32) + down_bias + summed).astype(jnp.bfloat16)


def solution(mesh):
    in_specs = (
        P(None, "lat", "lon", None),
        P(),
        P(),
        P(None, "ch", None, None),
        P(None, "ch", None),
        P(None, "ch", None, None),
        P(None, "ch", None),
        P(None, ("lat", "lon")),
        P(),
        P(),
        P(None, "ch"),
        P("ch"),
        P("ch", None),
        P("ch"),
    )
    out_specs = P(None, ("lat", "lon"), None, "ch")
    return jax.shard_map(shards, mesh=mesh, in_specs=in_specs, out_specs=out_specs, check_vma=False)
```

profile of v0, /device:TPU:8, one launch (start us, length us, event | category | flops | bytes accessed | tf_op | source)
XLA Modules:
  0.0 1580.2 jit_solution(13574943251398792839)
XLA Ops:
  6.5 9.7 convert_reduce_fusion.1
  16.3 0.1 copy.103
  16.4 2.4 copy-done.3
  18.8 6.7 fusion.17
  25.6 0.8 pad_maximum_fusion.4
  26.4 5.3 all-to-all-start.1
  31.7 8.4 constant_dynamic-slice_fusion
  40.1 0.0 all-to-all-done.1
  40.1 5.8 all-to-all-start
  46.0 0.1 dynamic_slice.10
  46.1 0.1 dynamic_slice.11
  46.1 5.0 multiply_convert_fusion.2
  51.2 1.6 copy.104
  52.8 1.7 all_to_all.46
  54.5 1.5 slice_bitcast_fusion.1
  55.9 192.2 %all-to-all-done = bf16[1,64,192,384]{3,2,0,1:T(8,128)(2,1)} async-done(((bf16[1,64,192,384]{3,2,0,1:T(8,128)(2,1)}), bf16[1,64,192,384]{3,2,0,1:T(8,128)(2,1)}, u32[]{:S(2)}, u32[]{:S(2)}) %all-to-all-start) | async-done | bytes 9437216 | tf_op jit(solution)/shard_map/all_to_all | solution.py:111
  248.2 12.7 convert_bitcast_fusion
  260.9 7.3 copy.102
  268.2 12.6 fusion.76
  280.8 0.0 copy-start.6
  280.8 0.0 copy-start.7
  280.8 8.9 copy.114
  289.7 8.6 all-to-all-start.2
  298.4 0.1 copy.152
  298.5 0.1 copy.151
  298.6 0.1 copy.150
  298.8 0.1 copy.149
  298.9 1.0 fusion.109
  299.9 1.1 negate_convert_fusion
  301.0 0.8 maximum_bitcast_fusion.14
  301.9 0.8 maximum_bitcast_fusion.12
  302.7 0.1 fusion.102
  302.8 198.3 %all-to-all-done.2 = bf16[1,1,16,2,16,24,384]{6,5,3,2,1,0,4:T(8,128)(2,1)} async-done(((bf16[1,1,16,2,16,24,384]{6,5,3,2,1,0,4:T(8,128)(2,1)}), bf16[1,1,16,2,16,24,384]{6,5,3,2,1,0,4:T(8,128)(2,1)}, u32[]{:S(2)}, u32[]{:S(2)}) %all-to-all-start.2) | async-done | bytes 9437216 | tf_op jit(solution)/shard_map/all_to_all | solution.py:126
  501.1 12.6 bitcast_convert_fusion.1
  513.6 8.9 fusion.57
  522.6 9.9 fusion.50
  532.5 8.6 copy.120
  541.1 11.3 bitcast_convert_fusion
  552.4 12.8 copy.122
  565.2 8.6 all-to-all-start.3
  573.8 0.0 all-gather.2.cloned.1.call-start
  573.8 5.3 multiply_convert_fusion.1
  579.2 18.7 %copy.106 = f32[1,16,768,384]{2,3,1,0:T(8,128)} copy(f32[1,16,768,384]{3,2,1,0:T(8,128)} %bitcast.161) | data formatting | bytes 37748736 | tf_op jit(solution)/shard_map/convert_element_type | solution.py:143
  597.9 178.8 %all-to-all-done.3 = bf16[1,16,16,2,1,24,384]{6,5,3,2,4,0,1:T(8,128)(2,1)} async-done(((bf16[1,16,16,2,1,24,384]{6,5,3,2,4,0,1:T(8,128)(2,1)}), bf16[1,16,16,2,1,24,384]{6,5,3,2,4,0,1:T(8,128)(2,1)}, u32[]{:S(2)}, u32[]{:S(2)}) %all-to-all-start.3) | async-done | bytes 9437216 | tf_op jit(solution)/shard_map/all_to_all | solution.py:138
  776.7 9.1 copy.123
  785.9 20.5 %fusion.51 = bf16[1,16,768,384]{2,3,1,0:T(8,128)(2,1)} fusion(f32[1,16,768,384]{2,3,1,0:T(8,128)} %copy.106, f32[384]{0:T(512)S(1)} %dynamic_slice.11, f32[384]{0:T(512)S(1)} %dynamic_slice.10, f32[16,768]{1,0:T(8,128)} %get-tuple-element.20, f32[16,768]{1,0:T(8,128)} %get-tuple-element.19, bf16[16,2,384,384]{3,2,1,0:T(8,128)(2,1)} %bitcast.164, ...), kind=kOutput, calls=%fused_computation.66 | convolution fusion | flops 7290814464 | bytes 39029760 | tf_op jit(solution)/shard_map/pkw,brpkc->brwc/dot_general | solution.py:140
  806.4 0.0 all-gather.2.cloned.1.call-update
  806.4 0.0 copy-start.15
  806.4 0.0 copy-start.16
  806.4 0.0 reduce-scatter.2.cloned.1.call-start
  806.5 226.5 %all-gather.2.cloned.1.call-done = bf16[1,16,768,768]{2,3,1,0:T(8,128)(2,1)} async-done(((bf16[1,16,768,384]{2,3,1,0:T(8,128)(2,1)}), bf16[1,16,768,768]{2,3,1,0:T(8,128)(2,1)}) %all-gather.2.cloned.1.call-update) | async-done | bytes 18874384 | tf_op jit(solution)/shard_map/all_gather | solution.py:146
  1032.9 8.0 convert_reduce_fusion
  1041.0 4.0 copy-done.2
  1044.9 5.2 fusion.12
  1050.2 12.0 fusion.15
  1062.3 24.7 %copy.125 = bf16[1,16,768,768]{3,2,1,0:T(8,128)(2,1)} copy(bf16[1,16,768,768]{2,3,1,0:T(8,128)(2,1)} %fusion.15) | data formatting | bytes 37748736 | tf_op jit(solution)/shard_map/convert_element_type | solution.py:151
  1087.0 188.0 %fusion.2.clone.6 = bf16[12288,1536]{1,0:T(8,128)(2,1)} fusion(bf16[12288,768]{1,0:T(8,128)(2,1)} %bitcast.162, bf16[768,1536]{1,0:T(8,128)(2,1)S(1)} %copy-done, f32[1536]{0:T(1024)S(1)} %copy-done.23), kind=kOutput, calls=%fused_computation.3.clone.clone.clone.clone.clone.1 | convolution fusion | flops 30236737536 | bytes 58988544 | tf_op jit(solution)/shard_map/dot_general | solution.py:155
  1275.0 36.2 %fusion.48 = bf16[12288,768]{1,0:T(8,128)(2,1)} fusion(bf16[1536,768]{1,0:T(8,128)(2,1)S(1)} %copy-done.22, bf16[12288,1536]{1,0:T(8,128)(2,1)} %fusion.2.clone.6), kind=kOutput, calls=%fused_computation.62 | convolution fusion | flops 29000466432 | bytes 58982400 | tf_op jit(solution)/shard_map/dot_general | solution.py:157
  1311.2 24.7 %copy.126 = bf16[1,16,768,768]{2,3,1,0:T(8,128)(2,1)} copy(bf16[1,16,768,768]{3,2,1,0:T(8,128)(2,1)} %bitcast.163) | data formatting | bytes 37748736 | tf_op jit(solution)/shard_map/convert_element_type | solution.py:161
  1335.9 0.0 reduce-scatter.2.cloned.1.call-update
  1335.9 0.0 copy-start.1
  1335.9 211.8 %reduce-scatter.2.cloned.1.call-done = bf16[1,16,768,384]{2,3,1,0:T(8,128)(2,1)} async-done(((bf16[1,16,768,768]{2,3,1,0:T(8,128)(2,1)}), bf16[1,16,768,384]{2,3,1,0:T(8,128)(2,1)}) %reduce-scatter.2.cloned.1.call-update) | async-done | bytes 9437200 | tf_op jit(solution)/shard_map/reduce_scatter | solution.py:160
  1547.8 12.5 add_convert_fusion
  1560.3 12.6 copy.127
  (54 shorter events, 0.3 us)
Async XLA Ops:
  6.5 1080.4 %copy-start = (bf16[768,1536]{1,0:T(8,128)(2,1)S(1)}, bf16[768,1536]{1,0:T(8,128)(2,1)}, u32[]{:S(2)}) copy-start(bf16[768,1536]{1,0:T(8,128)(2,1)} %param.24) | copy-start | bytes 7077892
  6.5 12.3 copy-start.3
  26.4 13.7 all-to-all-start.1
  31.7 14.3 copy-start.20
  31.7 14.4 copy-start.21
  40.1 5.9 copy-start.5
  40.1 208.0 %all-to-all-start = ((bf16[1,64,192,384]{3,2,0,1:T(8,128)(2,1)}), bf16[1,64,192,384]{3,2,0,1:T(8,128)(2,1)}, u32[]{:S(2)}, u32[]{:S(2)}) async-start(bf16[1,64,192,384]{3,2,0,1:T(8,128)(2,1)} %constant_dynamic-slice_fusion), calls=%async_computation | async-start | bytes 18874368 | tf_op jit(solution)/shard_map/all_to_all | solution.py:111
  260.9 7.3 copy-start.12
  260.9 7.3 copy-start.13
  268.2 12.6 copy-start.4
  280.8 17.5 %copy-start.17 = (f32[2,4,96]{2,1,0:T(4,128)S(1)}, f32[2,4,96]{2,1,0:T(4,128)}, u32[]{:S(2)}) copy-start(f32[2,4,96]{2,1,0:T(4,128)} %param.18) | copy-start | bytes 9220
  280.8 17.5 %copy-start.18 = (f32[2,4,96]{2,1,0:T(4,128)S(1)}, f32[2,4,96]{2,1,0:T(4,128)}, u32[]{:S(2)}) copy-start(f32[2,4,96]{2,1,0:T(4,128)} %param.20) | copy-start | bytes 9220
  280.8 17.5 %copy-start.14 = (s32[256,24]{0,1:T(8,128)S(1)}, s32[256,24]{0,1:T(8,128)}, u32[]{:S(2)}) copy-start(s32[256,24]{0,1:T(8,128)} %param.21) | copy-start | bytes 73732
  280.8 17.5 %copy-start.6 = (bf16[2,4,96,96]{3,2,1,0:T(8,128)(2,1)S(1)}, bf16[2,4,96,96]{3,2,1,0:T(8,128)(2,1)}, u32[]{:S(2)}) copy-start(bf16[2,4,96,96]{3,2,1,0:T(8,128)(2,1)} %param.17) | copy-start | bytes 442372
  280.8 17.8 %copy-start.7 = (bf16[2,4,96,96]{3,2,1,0:T(8,128)(2,1)S(1)}, bf16[2,4,96,96]{3,2,1,0:T(8,128)(2,1)}, u32[]{:S(2)}) copy-start(bf16[2,4,96,96]{3,2,1,0:T(8,128)(2,1)} %param.19) | copy-start | bytes 442372
  289.7 211.4 %all-to-all-start.2 = ((bf16[1,1,16,2,16,24,384]{6,5,3,2,1,0,4:T(8,128)(2,1)}), bf16[1,1,16,2,16,24,384]{6,5,3,2,1,0,4:T(8,128)(2,1)}, u32[]{:S(2)}, u32[]{:S(2)}) async-start(bf16[1,1,16,2,16,24,384]{6,5,3,2,1,0,4:T(8,128)(2,1)} %copy.114), calls=%async_computation.2 | async-start | bytes 18874368 | tf_op jit(solution)/shard_map/all_to_all | solution.py:126
  501.1 12.6 copy-start.8
  501.1 12.6 copy-start.9
  513.6 8.9 copy-start.10
  513.6 8.9 copy-start.11
  565.2 211.5 %all-to-all-start.3 = ((bf16[1,16,16,2,1,24,384]{6,5,3,2,4,0,1:T(8,128)(2,1)}), bf16[1,16,16,2,1,24,384]{6,5,3,2,4,0,1:T(8,128)(2,1)}, u32[]{:S(2)}, u32[]{:S(2)}) async-start(bf16[1,16,16,2,1,24,384]{6,5,3,2,4,0,1:T(8,128)(2,1)} %copy.122), calls=%async_computation.3 | async-start | bytes 18874368 | tf_op jit(solution)/shard_map/all_to_all | solution.py:138
  573.8 459.1 %all-gather.2.cloned.1.call-start = ((), (), s32[]{:S(2)}) async-start(), calls=%async_computation.5 | async-start | bytes 28311552 | tf_op jit(solution)/shard_map/all_gather | solution.py:146
  806.4 243.8 %copy-start.15 = (f32[768]{0:T(1024)S(1)}, f32[768]{0:T(1024)}, u32[]{:S(2)}) copy-start(f32[768]{0:T(1024)} %param.23) | copy-start | bytes 9220
  806.4 243.8 %copy-start.16 = (f32[768]{0:T(1024)S(1)}, f32[768]{0:T(1024)}, u32[]{:S(2)}) copy-start(f32[768]{0:T(1024)} %param.22) | copy-start | bytes 9220
  806.4 741.3 %reduce-scatter.2.cloned.1.call-start = ((), (), s32[]{:S(2)}) async-start(), calls=%async_computation.6 | async-start | bytes 28311552 | tf_op jit(solution)/shard_map/reduce_scatter | solution.py:160
  1032.9 12.0 copy-start.2
  1062.3 24.7 %copy-start.23 = (f32[1536]{0:T(1024)S(1)}, f32[1536]{0:T(1024)}, u32[]{:S(2)}) copy-start(f32[1536]{0:T(1024)} %param.25) | copy-start | bytes 18436
  1087.0 188.0 %copy-start.22 = (bf16[1536,768]{1,0:T(8,128)(2,1)S(1)}, bf16[1536,768]{1,0:T(8,128)(2,1)}, u32[]{:S(2)}) copy-start(bf16[1536,768]{1,0:T(8,128)(2,1)} %param.26) | copy-start | bytes 7077892
  1335.9 211.9 %copy-start.19 = (f32[384]{0:T(512)S(1)}, f32[384]{0:T(512)}, u32[]{:S(2)}) copy-start(f32[384]{0:T(512)} %param.27) | copy-start | bytes 4612
  1335.9 236.9 %copy-start.1 = (bf16[768,1536]{1,0:T(8,128)(2,1)S(1)}, bf16[768,1536]{1,0:T(8,128)(2,1)}, u32[]{:S(2)}) copy-start(bf16[768,1536]{1,0:T(8,128)(2,1)} %param.24) | copy-start | bytes 7077892
Sparse Core Ops, SparseCore 0:
  806.5 226.3 all-gather.1
  1336.0 211.6 reduce-scatter.1
where the time goes:
time: 1590 us; the launch traced here: 1580 us
  waiting for transfers between devices  1010 us (64%)
  matrix products  300 us (19%)
  local copies, waits for them, and re-layouts  148 us (9%)
  other arithmetic  82 us (5%)
  starting transfers between devices  28.4 us (2%)
    all_gather x1, waiting for transfers between devices, shards(): lax.all_gather(mixed, 'ch', axis=3, tiled=True).astype(jnp.float32)  226 us
    reduce_scatter x1, waiting for transfers between devices, shards(): lax.psum_scatter(partial_rows.astype(jnp.bfloat16), 'ch', scatter_dimensi...  212 us
    all_to_all x1, waiting for transfers between devices, shards(): lax.all_to_all(packed, ('lat', 'lon'), split_axis=4, concat_axis=1, tiled...  198 us
    all_to_all x1, waiting for transfers between devices, shards(): lax.all_to_all(token_part, 'lon', split_axis=1, concat_axis=2, tiled=True)  192 us
    dot_general x1, matrix products, shards(): jnp.dot(tokens, up_weight, preferred_element_type=jnp.float32) + up_bias  188 us
    all_to_all x1, waiting for transfers between devices, shards(): lax.all_to_all(packed_back, ('lat', 'lon'), split_axis=1, concat_axis=4,...  179 us
    dot_general x1, matrix products, shards(): jnp.dot(hidden, down_weight, preferred_element_type=jnp.float32)  36.2 us
  transfers between devices with their start and end apart: 6, of which 5 were waited for; matrix products, arithmetic and copies ran while one was open for 3% of the time, Pallas kernels for 0%

commit v1 on v0

--- a/solution.py
+++ b/solution.py
@@ -7,6 +7,8 @@
 
 shrink_level = 0.01
 norm_epsilon = 1e-05
+step_limit = 4
+block_total = 8
 
 
 def lon_tables(lon_width, mode_count):
@@ -74,7 +76,7 @@
     )
 
 
-def shards(
+def dense_shards(
     grid_tokens,
     first_gain,
     first_bias,
@@ -163,6 +165,158 @@
     return (mixed.astype(jnp.float32) + down_bias + summed).astype(jnp.bfloat16)
 
 
+def gelu(values):
+    return 0.5 * values * (1.0 + lax.erf(values * math.sqrt(0.5)))
+
+
+def block_shards(
+    grid_tokens,
+    first_gain,
+    first_bias,
+    first_filter,
+    first_shift,
+    second_filter,
+    second_shift,
+    mode_mask,
+    second_gain,
+    second_bias,
+    up_weight,
+    up_bias,
+    down_weight,
+    down_bias,
+):
+    lats = lax.axis_size("lat")
+    lons = lax.axis_size("lon")
+    chs = lax.axis_size("ch")
+    _, rows_here, cols_here, channels = grid_tokens.shape
+    width = cols_here * lons
+    height = rows_here * lats
+    modes = width // 2
+    modes_here = modes // lats
+    part = channels // chs
+    own = part // lons
+    blocks_here = first_filter.shape[1] // lons
+    ch_at = lax.axis_index("ch")
+    lon_at = lax.axis_index("lon")
+    steps = math.gcd(step_limit, rows_here // (lons * chs))
+    line = rows_here // (lons * chs * steps)
+    rows = chs * lons * line
+
+    up_all = lax.all_gather(up_weight, "ch", axis=1, tiled=True)
+    down_all = lax.all_gather(down_weight, "ch", axis=0, tiled=True)
+    biases = lax.all_gather(jnp.concatenate([up_bias, down_bias]), "ch", axis=0, tiled=False)
+    up_shift = biases[:, : up_bias.shape[0]].reshape(-1)
+    down_shift = biases[:, up_bias.shape[0] :].reshape(-1)
+    keep_mask = lax.all_gather(mode_mask, "lon", axis=1, tiled=True)
+
+    tokens = grid_tokens[0]
+    token_part = lax.dynamic_slice_in_dim(tokens, ch_at * part, part, 2)
+    token_part = token_part.reshape(lons, chs, steps, line, cols_here, lons, own)
+    arrived = []
+    for step in range(steps):
+        sent = jnp.transpose(token_part[:, :, step], (4, 3, 1, 0, 2, 5))
+        sent = sent.reshape(lons, cols_here, rows * own)
+        sent = lax.all_to_all(sent, "lon", split_axis=0, concat_axis=0, tiled=True)
+        arrived.append(sent.reshape(width, rows, own))
+
+    values = tokens.astype(jnp.float32)
+    center = jnp.mean(values, axis=-1, keepdims=True)
+    inv_dev = lax.rsqrt(
+        jnp.mean(jnp.square(values - center), axis=-1, keepdims=True) + norm_epsilon
+    )
+    moments = jnp.stack([center[..., 0].T, inv_dev[..., 0].T])
+    moments = lax.all_gather(moments, "lon", axis=1, tiled=True)
+    moments = moments.reshape(2, width, lons, chs, steps, line)
+    moments = jnp.transpose(moments, (4, 0, 1, 3, 2, 5)).reshape(steps, 2, width, rows, 1)
+    own_at = ch_at * part + lon_at * own
+    gain_part = lax.dynamic_slice_in_dim(first_gain, own_at, own, 0)
+    bias_part = lax.dynamic_slice_in_dim(first_bias, own_at, own, 0)
+
+    lon_forward, lon_inverse = lon_tables(width, modes)
+    lat_forward, lat_inverse = lat_tables(height)
+    shape = (2, 2, height, lats, lons, chs, steps, line)
+    order = (6, 3, 1, 5, 4, 7, 0, 2)
+    lat_forward = jnp.transpose(lat_forward.reshape(shape), order).reshape(
+        steps, lats, 2, rows, 2, height
+    )
+    lat_inverse = jnp.swapaxes(lat_inverse, 2, 3).reshape(shape)
+    lat_inverse = jnp.transpose(lat_inverse, (6, 3, 0, 5, 4, 7, 1, 2)).reshape(
+        steps, lats, 2, rows, 2, height
+    )
+    lon_inverse = jnp.swapaxes(lon_inverse.reshape(2, lats, modes_here, width), 0, 1)
+
+    base = []
+    spectra = []
+    for step in range(steps):
+        token_rows = arrived[step].astype(jnp.float32)
+        normed = (
+            (token_rows - moments[step, 0]) * moments[step, 1] * gain_part + bias_part
+        ).astype(jnp.bfloat16)
+        base.append((arrived[step], normed))
+        sent = jnp.einsum("pkw,whc->phkc", lon_forward, normed, preferred_element_type=jnp.float32)
+        sent = sent.astype(jnp.bfloat16).reshape(2, rows, lats, modes_here, own)
+        sent = jnp.transpose(sent, (2, 0, 1, 3, 4)).reshape(lats, 2 * rows, modes_here * own)
+        sent = lax.all_to_all(sent, "lat", split_axis=0, concat_axis=0, tiled=True)
+        spectra.append(sent)
+    spectrum_rows = jnp.concatenate(spectra, axis=0).reshape(
+        steps, lats, 2, rows, modes_here, own
+    )
+    spectrum = jnp.einsum(
+        "jlphxq,jlphkc->xqkc", lat_forward, spectrum_rows, preferred_element_type=jnp.float32
+    ).astype(jnp.bfloat16)
+    pick = lambda array: lax.dynamic_slice_in_dim(array, lon_at * blocks_here, blocks_here, 1)
+    filtered_modes = mode_mixer(
+        spectrum[None],
+        pick(first_filter),
+        pick(first_shift),
+        pick(second_filter),
+        pick(second_shift),
+        keep_mask,
+    )[0]
+
+    returned = []
+    for step in range(steps):
+        sent = jnp.einsum(
+            "lyhxq,xqkc->lykhc",
+            lat_inverse[step],
+            filtered_modes,
+            preferred_element_type=jnp.float32,
+        )
+        sent = sent.astype(jnp.bfloat16).reshape(lats, 2 * modes_here, rows * own)
+        sent = lax.all_to_all(sent, "lat", split_axis=0, concat_axis=0, tiled=True)
+        returned.append(sent.reshape(lats, 2, modes_here, rows, own))
+
+    results = []
+    for step in range(steps):
+        filtered = jnp.einsum(
+            "lykw,lykhc->hcw", lon_inverse, returned[step], preferred_element_type=jnp.float32
+        )
+        token_rows, normed = base[step]
+        kept = token_rows.astype(jnp.float32) + normed.astype(jnp.float32)
+        mixed = (jnp.transpose(kept, (1, 2, 0)) + filtered).astype(jnp.bfloat16)
+        mixed = mixed.reshape(chs * lons, line * own, width)
+        mixed = lax.all_to_all(mixed, ("ch", "lon"), split_axis=0, concat_axis=0, tiled=True)
+        mixed = jnp.swapaxes(mixed.reshape(chs * lons, line, own, width), 0, 1)
+        mixed = mixed.reshape(line, channels, width)
+        all_channels = mixed.astype(jnp.float32)
+        center_two = jnp.mean(all_channels, axis=1, keepdims=True)
+        inv_two = lax.rsqrt(
+            jnp.mean(jnp.square(all_channels - center_two), axis=1, keepdims=True) + norm_epsilon
+        )
+        normed_two = (
+            (all_channels - center_two) * inv_two * second_gain[:, None] + second_bias[:, None]
+        ).astype(jnp.bfloat16)
+        hidden = jnp.einsum("icw,cj->iwj", normed_two, up_all, preferred_element_type=jnp.float32)
+        hidden = gelu(hidden + up_shift).astype(jnp.bfloat16)
+        total = jnp.einsum("iwj,jc->iwc", hidden, down_all, preferred_element_type=jnp.float32)
+        total = total + down_shift + jnp.swapaxes(mixed, 1, 2).astype(jnp.float32)
+        total = total.astype(jnp.bfloat16).reshape(line * width, chs, part)
+        sent = jnp.swapaxes(total, 0, 1)
+        sent = lax.all_to_all(sent, "ch", split_axis=0, concat_axis=0, tiled=True)
+        results.append(sent.reshape(chs, line, width, part))
+    return jnp.stack(results, axis=1).reshape(1, chs * steps * line, width, part)
+
+
 def solution(mesh):
     in_specs = (
         P(None, "lat", "lon", None),
@@ -181,4 +335,7 @@
         P("ch"),
     )
     out_specs = P(None, ("lat", "lon"), None, "ch")
+    blocks_here = block_total // mesh.shape["ch"]
+    fits = blocks_here % mesh.shape["lon"] == 0
+    shards = block_shards if fits else dense_shards
     return jax.shard_map(shards, mesh=mesh, in_specs=in_specs, out_specs=out_specs, check_vma=False)

time: 1590 us -> 1200 us (0.75)
  waiting for transfers between devices: 1010 us -> 297 us
  local copies, waits for them, and re-layouts: 148 us -> 382 us
  blocking collectives: 0 us -> 97 us
  matrix products: 300 us -> 206 us
  starting transfers between devices: 28.4 us -> 110 us
    all_to_all x4 -> x19, waiting for transfers between devices: 569 us -> 256 us  [the longest x4 103 us: block_shards(): sent = lax.all_to_all(sent, 'lon', split_axis=0, concat_axis=0, tiled=True)]
    reduce_scatter x1 -> x0, waiting for transfers between devices: 212 us -> none  [shards(): lax.psum_scatter(partial_rows.astype(jnp.bfloat16), 'ch', scatter_dimensi...]
    reshape x2 -> x34, local copies, waits for them, and re-layouts: 21.7 us -> 227 us  [the longest x8 40.3 us: block_shards(): sent = sent.astype(jnp.bfloat16).reshape(2, rows, lats, modes_here, own)]
    all_gather x1 -> x2, waiting for transfers between devices: 226 us -> 38.9 us  [the longest x1 38.9 us: block_shards(): down_all = lax.all_gather(down_weight, 'ch', axis=0, tiled=True)]
    dot_general x6 -> x16, matrix products: 281 us -> 180 us  [the longest x4 96.5 us: block_shards(): jnp.einsum('iwj,jc->iwc', hidden, down_all, preferred_element_type=jnp.fl...]
    all_to_all x4 -> x19, starting transfers between devices: 28.3 us -> 110 us  [the longest x8 34.9 us: block_shards(): sent = lax.all_to_all(sent, 'lat', split_axis=0, concat_axis=0, tiled=True)]
    all_gather x0 -> x3, blocking collectives: none -> 66 us  [the longest x1 43.6 us: block_shards(): moments = lax.all_gather(moments, 'lon', axis=1, tiled=True)]
    transpose x0 -> x8, local copies, waits for them, and re-layouts: none -> 35.5 us  [the longest x5 34.3 us: block_shards(): sent = jnp.transpose(token_part[:, :, step], (4, 3, 1, 0, 2, 5))]
  transfers between devices with their start and end apart: 6 -> 21, of which waited for: 5 -> 13; matrix products, arithmetic and copies ran while one was open for 3% -> 45% of each run, Pallas kernels for 0% -> 0%
where the time goes in v1:
time: 1200 us; the launch traced here: 1190 us
  local copies, waits for them, and re-layouts  382 us (32%)
  waiting for transfers between devices  297 us (25%)
  matrix products  206 us (17%)
  starting transfers between devices  110 us (9%)
  blocking collectives  97 us (8%)
  other arithmetic  81.2 us (7%)
  between operations  14.7 us (1%)
    all_to_all x4, waiting for transfers between devices, block_shards(): sent = lax.all_to_all(sent, 'lon', split_axis=0, concat_axis=0, tiled=True)  103 us
    dot_general x4, matrix products, block_shards(): jnp.einsum('iwj,jc->iwc', hidden, down_all, preferred_element_type=jnp.fl...  96.5 us
    all_to_all x4, waiting for transfers between devices, block_shards(): lax.all_to_all(mixed, ('ch', 'lon'), split_axis=0, concat_axis=0, tiled=T...  80.9 us
    all_to_all x8, waiting for transfers between devices, block_shards(): sent = lax.all_to_all(sent, 'lat', split_axis=0, concat_axis=0, tiled=True)  60 us
    all_gather x1, blocking collectives, block_shards(): moments = lax.all_gather(moments, 'lon', axis=1, tiled=True)  43.6 us
    reshape x8, local copies, waits for them, and re-layouts, block_shards(): sent = sent.astype(jnp.bfloat16).reshape(2, rows, lats, modes_here, own)  40.3 us
    reshape x4, local copies, waits for them, and re-layouts, block_shards(): sent = sent.reshape(lons, cols_here, rows * own)  39.1 us
    all_gather x1, waiting for transfers between devices, block_shards(): down_all = lax.all_gather(down_weight, 'ch', axis=0, tiled=True)  38.9 us
  transfers between devices with their start and end apart: 21, of which 13 were waited for; matrix products, arithmetic and copies ran while one was open for 45% of the time, Pallas kernels for 0%

profile of v1, /device:TPU:8, one launch (start us, length us, event | category | flops | bytes accessed | tf_op | source)
XLA Modules:
  0.0 1188.2 jit_solution(13620815806632485575)
XLA Ops:
  6.5 8.4 constant_dynamic-slice_fusion.6
  14.9 23.4 %reshape.589 = bf16[4,2,4,2,192,4,96]{6,5,4,3,2,1,0:T(4,128)(2,1)} reshape(bf16[1,64,192,384]{3,2,1,0:T(8,128)(2,1)} %constant_dynamic-slice_fusion.6) | data formatting | bytes 18874368 | tf_op jit(solution)/shard_map/reshape | solution.py:214
  38.3 11.1 slice_bitcast_fusion.3
  54.2 9.8 reshape.590
  69.5 6.7 copy.439
  76.2 9.8 reshape.598
  86.0 34.0 %all-to-all-done = bf16[4,192,1536]{2,1,0:T(8,128)(2,1)} async-done(((bf16[4,192,1536]{2,1,0:T(8,128)(2,1)}), bf16[4,192,1536]{2,1,0:T(8,128)(2,1)}, u32[]{:S(2)}, u32[]{:S(2)}) %all-to-all-start) | async-done | bytes 2359328 | tf_op jit(solution)/shard_map/all_to_all | solution.py:219
  120.0 7.9 all-to-all-start.2
  127.9 6.7 copy.442
  134.6 9.8 reshape.601
  144.4 33.6 %all-to-all-done.2 = bf16[4,192,1536]{2,1,0:T(8,128)(2,1)} async-done(((bf16[4,192,1536]{2,1,0:T(8,128)(2,1)}), bf16[4,192,1536]{2,1,0:T(8,128)(2,1)}, u32[]{:S(2)}, u32[]{:S(2)}) %all-to-all-start.2) | async-done | bytes 2359328 | tf_op jit(solution)/shard_map/all_to_all | solution.py:219
  177.9 8.1 all-to-all-start.4
  191.0 9.8 reshape.604
  200.7 35.3 %all-to-all-done.4 = bf16[4,192,1536]{2,1,0:T(8,128)(2,1)} async-done(((bf16[4,192,1536]{2,1,0:T(8,128)(2,1)}), bf16[4,192,1536]{2,1,0:T(8,128)(2,1)}, u32[]{:S(2)}, u32[]{:S(2)}) %all-to-all-start.4) | async-done | bytes 2359328 | tf_op jit(solution)/shard_map/all_to_all | solution.py:219
  236.1 7.8 all-to-all-start.6
  243.9 9.3 convert_reduce_fusion
  254.8 11.3 fusion.2
  266.2 43.6 %all_gather.18 = f32[2,768,64]{2,0,1:T(2,128)S(1)} all-gather(f32[2,192,64]{2,0,1:T(2,128)S(1)} %copy.428), channel_id=1, replica_groups=mesh['lat'=4,'lon'=4,'ch'=2] {'lon'}, dimensions={1}, use_global_device_ids=true | all-gather | bytes 491520 | tf_op jit(solution)/shard_map/all_gather | solution.py:228
  315.7 6.4 reshape.627
  328.3 6.3 convert_bitcast_fusion.8
  344.7 6.7 reshape.597
  356.0 6.3 reshape.628
  362.3 6.3 copy.440
  368.7 6.3 convert_bitcast_fusion.7
  385.1 6.7 reshape.600
  396.5 6.3 reshape.629
  402.8 6.3 copy.443
  409.2 6.3 convert_bitcast_fusion.6
  425.6 6.7 reshape.603
  448.6 6.3 copy.446
  455.0 6.3 convert_bitcast_fusion.5
  471.4 6.7 reshape.606
  484.2 13.6 %all_gather.19 = s32[256,96]{0,1:T(8,128)S(1)} all-gather(s32[256,24]{0,1:T(8,128)S(1)} %copy-done.29), channel_id=1, replica_groups=mesh['lat'=4,'lon'=4,'ch'=2] {'lon'}, dimensions={1}, use_global_device_ids=true | all-gather | bytes 122880 | tf_op jit(solution)/shard_map/all_gather | solution.py:210
  510.3 8.3 pad_maximum_fusion
  518.7 18.7 %reshape.607 = bf16[4,4,2,16,96,96]{5,4,3,2,1,0:T(8,128)(2,1)} reshape(bf16[16,32,9216]{2,1,0:T(8,128)(2,1)} %pad_maximum_fusion) | data formatting | bytes 18874368 | tf_op jit(solution)/shard_map/reshape | solution.py:261
  537.4 20.2 %fusion.13 = bf16[2,256,96,96]{1,3,2,0:T(8,128)(2,1)} fusion(f32[2,96]{1,0:T(2,128)S(1)} %bitcast.485, bf16[4,4,2,16,96,96,1]{5,4,3,2,1,0,6:T(8,128)(2,1)} %bitcast.463, bf16[4,4,2,16,2,256]{5,4,3,2,1,0:T(2,128)(2,1)S(1)} %bitcast.477, bf16[1,1,96,2,96]{2,4,0,3,1:T(8,128)(2,1)S(1)} %copy-done.26, bf16[1,1,96,2,96]{2,4,0,3,1:T(8,128)(2,1)S(1)} %copy-done.25), kind=kOutput, calls=%fused_computation.22 | convolution fusion | flops 6662799360 | bytes 19473152 | tf_op jit(solution)/shard_map/bpxyni,pniqo->bqxyno/dot_general | solution.py:56
  557.6 6.5 fusion.14
  578.3 7.5 fusion.61
  590.8 15.9 %all-to-all-done.8 = bf16[4,192,1536]{2,1,0:T(8,128)(2,1)} async-done(((bf16[4,192,1536]{2,1,0:T(8,128)(2,1)}), bf16[4,192,1536]{2,1,0:T(8,128)(2,1)}, u32[]{:S(2)}, u32[]{:S(2)}) %all-to-all-start.8) | async-done | bytes 2359328 | tf_op jit(solution)/shard_map/all_to_all | solution.py:286
  611.4 7.5 fusion.62
  624.0 15.8 %all-to-all-done.11 = bf16[4,192,1536]{2,1,0:T(8,128)(2,1)} async-done(((bf16[4,192,1536]{2,1,0:T(8,128)(2,1)}), bf16[4,192,1536]{2,1,0:T(8,128)(2,1)}, u32[]{:S(2)}, u32[]{:S(2)}) %all-to-all-start.11) | async-done | bytes 2359328 | tf_op jit(solution)/shard_map/all_to_all | solution.py:286
  644.7 7.5 fusion.63
  657.2 15.8 %all-to-all-done.14 = bf16[4,192,1536]{2,1,0:T(8,128)(2,1)} async-done(((bf16[4,192,1536]{2,1,0:T(8,128)(2,1)}), bf16[4,192,1536]{2,1,0:T(8,128)(2,1)}, u32[]{:S(2)}, u32[]{:S(2)}) %all-to-all-start.14) | async-done | bytes 2359328 | tf_op jit(solution)/shard_map/all_to_all | solution.py:286
  688.3 7.5 fusion.43
  695.8 9.4 all-to-all-done.17
  719.7 8.3 fusion.42
  728.0 35.1 %all-to-all-done.9 = bf16[8,192,768]{2,1,0:T(8,128)(2,1)S(1)} async-done(((bf16[8,192,768]{2,1,0:T(8,128)(2,1)}), bf16[8,192,768]{2,1,0:T(8,128)(2,1)S(1)}, u32[]{:S(2)}, u32[]{:S(2)}) %all-to-all-start.9) | async-done | bytes 2359328 | tf_op jit(solution)/shard_map/all_to_all | solution.py:298
  764.5 8.3 all-to-all-start.12
  778.8 7.5 fusion.41
  786.4 35.5 %all-to-all-done.12 = bf16[8,192,768]{2,1,0:T(8,128)(2,1)S(1)} async-done(((bf16[8,192,768]{2,1,0:T(8,128)(2,1)}), bf16[8,192,768]{2,1,0:T(8,128)(2,1)S(1)}, u32[]{:S(2)}, u32[]{:S(2)}) %all-to-all-start.12) | async-done | bytes 2359328 | tf_op jit(solution)/shard_map/all_to_all | solution.py:298
  821.9 8.6 all-to-all-start.15
  831.3 8.9 all-gather.1
  847.0 7.8 fusion.40
  868.5 10.3 all-to-all-done.15
  878.8 9.2 all-to-all-start.18
  897.2 38.9 %all-gather.7.cloned.1.call-done = bf16[3072,768]{1,0:T(8,128)(2,1)} async-done(((bf16[1536,768]{1,0:T(8,128)(2,1)}), bf16[3072,768]{1,0:T(8,128)(2,1)}) %all-gather.7.cloned.1.call-update) | async-done | bytes 4718608 | tf_op jit(solution)/shard_map/all_gather | solution.py:206
  936.1 24.1 %fusion.47 = bf16[2,768,768]{2,1,0:T(8,128)(2,1)} fusion(f32[2,768,768]{1,2,0:T(8,128)} %copy.458, bf16[3072,768]{1,0:T(8,128)(2,1)} %all-gather.7.cloned.1.call-done, f32[3072]{0:T(1024)S(1)} %copy-done.30, bf16[768,3072]{1,0:T(8,128)(2,1)} %all-gather.5.cloned.1.call-done, f32[2,768,768]{2,1,0:T(8,128)} %bitcast.452, f32[768]{0:T(1024)S(1)} %add.371, ...), kind=kOutput, calls=%fused_computation.63 | convolution fusion | flops 14533263360 | bytes 21267456 | tf_op jit(solution)/shard_map/iwj,jc->iwc/dot_general | solution.py:311
  992.1 24.1 %fusion.46 = bf16[2,768,768]{2,1,0:T(8,128)(2,1)} fusion(f32[2,768,768]{1,2,0:T(8,128)} %copy.467, bf16[3072,768]{1,0:T(8,128)(2,1)} %all-gather.7.cloned.1.call-done, f32[3072]{0:T(1024)S(1)} %copy-done.30, bf16[768,3072]{1,0:T(8,128)(2,1)} %all-gather.5.cloned.1.call-done, f32[2,768,768]{2,1,0:T(8,128)} %bitcast.458, f32[2,768]{1,0:T(2,128)S(1)} %add_rsqrt_fusion.2, ...), kind=kOutput, calls=%fused_computation.60 | convolution fusion | flops 14533263360 | bytes 21267456 | tf_op jit(solution)/shard_map/iwj,jc->iwc/dot_general | solution.py:311
  1020.0 24.3 %fusion.45 = bf16[2,768,768]{2,1,0:T(8,128)(2,1)} fusion(f32[2,768,768]{1,2,0:T(8,128)} %copy.476, bf16[3072,768]{1,0:T(8,128)(2,1)} %all-gather.7.cloned.1.call-done, f32[3072]{0:T(1024)S(1)} %copy-done.30, bf16[768,3072]{1,0:T(8,128)(2,1)} %all-gather.5.cloned.1.call-done, f32[2,768,768]{2,1,0:T(8,128)} %bitcast.454, f32[2,768]{1,0:T(2,128)S(1)} %add_rsqrt_fusion.1, ...), kind=kOutput, calls=%fused_computation.57 | convolution fusion | flops 14533263360 | bytes 21267456 | tf_op jit(solution)/shard_map/iwj,jc->iwc/dot_general | solution.py:311
  1083.0 12.7 %all-to-all-done.13 = bf16[2,1536,384]{2,1,0:T(8,128)(2,1)} async-done(((bf16[2,1536,384]{2,1,0:T(8,128)(2,1)}), bf16[2,1536,384]{2,1,0:T(8,128)(2,1)}, u32[]{:S(2)}, u32[]{:S(2)}) %all-to-all-start.13) | async-done | bytes 2359328 | tf_op jit(solution)/shard_map/all_to_all | solution.py:315
  1100.6 24.1 %fusion.44 = bf16[2,768,768]{2,1,0:T(8,128)(2,1)} fusion(f32[2,768,768]{1,2,0:T(8,128)} %copy.485, bf16[3072,768]{1,0:T(8,128)(2,1)} %all-gather.7.cloned.1.call-done, f32[3072]{0:T(1024)S(1)} %copy-done.30, bf16[768,3072]{1,0:T(8,128)(2,1)} %all-gather.5.cloned.1.call-done, f32[2,768,768]{2,1,0:T(8,128)} %bitcast.456, f32[2,768]{1,0:T(2,128)S(1)} %add_rsqrt_fusion, ...), kind=kOutput, calls=%fused_computation.54 | convolution fusion | flops 14533263360 | bytes 21267456 | tf_op jit(solution)/shard_map/iwj,jc->iwc/dot_general | solution.py:311
  1133.9 31.0 %all_to_all.100 = bf16[2,1536,384]{2,1,0:T(8,128)(2,1)S(1)} all-to-all(bf16[2,1536,384]{2,1,0:T(8,128)(2,1)} %bitcast.469), channel_id=1, replica_groups=mesh['lat'=4,'lon'=4,'ch'=2] {'ch'}, dimensions={0} | all-to-all | bytes 4718592 | tf_op jit(solution)/shard_map/all_to_all | solution.py:315
  1164.8 7.5 pad_maximum_fusion.1
  1172.3 8.7 copy.487
  (217 shorter events, 308.4 us)
Async XLA Ops:
  6.5 495.6 %copy-start = (f32[2,4,96]{2,1,0:T(4,128)S(1)}, f32[2,4,96]{2,1,0:T(4,128)}, u32[]{:S(2)}) copy-start(f32[2,4,96]{2,1,0:T(4,128)} %param.18) | copy-start | bytes 9220
  64.0 56.0 %all-to-all-start = ((bf16[4,192,1536]{2,1,0:T(8,128)(2,1)}), bf16[4,192,1536]{2,1,0:T(8,128)(2,1)}, u32[]{:S(2)}, u32[]{:S(2)}) async-start(bf16[4,192,1536]{2,1,0:T(8,128)(2,1)} %reshape.590), calls=%async_computation | async-start | bytes 4718592 | tf_op jit(solution)/shard_map/all_to_all | solution.py:219
  120.0 57.9 %all-to-all-start.2 = ((bf16[4,192,1536]{2,1,0:T(8,128)(2,1)}), bf16[4,192,1536]{2,1,0:T(8,128)(2,1)}, u32[]{:S(2)}, u32[]{:S(2)}) async-start(bf16[4,192,1536]{2,1,0:T(8,128)(2,1)} %reshape.598), calls=%async_computation.2 | async-start | bytes 4718592 | tf_op jit(solution)/shard_map/all_to_all | solution.py:219
  177.9 58.1 %all-to-all-start.4 = ((bf16[4,192,1536]{2,1,0:T(8,128)(2,1)}), bf16[4,192,1536]{2,1,0:T(8,128)(2,1)}, u32[]{:S(2)}, u32[]{:S(2)}) async-start(bf16[4,192,1536]{2,1,0:T(8,128)(2,1)} %reshape.601), calls=%async_computation.4 | async-start | bytes 4718592 | tf_op jit(solution)/shard_map/all_to_all | solution.py:219
  236.1 115.3 %all-to-all-start.6 = ((bf16[4,192,1536]{2,1,0:T(8,128)(2,1)}), bf16[4,192,1536]{2,1,0:T(8,128)(2,1)}, u32[]{:S(2)}, u32[]{:S(2)}) async-start(bf16[4,192,1536]{2,1,0:T(8,128)(2,1)} %reshape.604), calls=%async_computation.6 | async-start | bytes 4718592 | tf_op jit(solution)/shard_map/all_to_all | solution.py:219
  254.0 524.8 %copy-start.35 = (f32[96]{0:T(128)}, f32[96]{0:T(128)S(1)}, u32[]{:S(2)}) copy-start(f32[96]{0:T(128)S(1)} %dynamic_slice.22) | copy-start | bytes 1156
  254.8 524.1 %copy-start.36 = (f32[96]{0:T(128)}, f32[96]{0:T(128)S(1)}, u32[]{:S(2)}) copy-start(f32[96]{0:T(128)S(1)} %dynamic_slice.23) | copy-start | bytes 1156
  315.3 12.9 %copy-start.6 = (bf16[1,384,768]{2,1,0:T(8,128)(2,1)}, bf16[1,384,768]{2,1,0:T(8,128)(2,1)S(1)}, u32[]{:S(2)}) copy-start(bf16[1,384,768]{2,1,0:T(8,128)(2,1)S(1)} %get-tuple-element.50) | copy-start | bytes 1769476
  315.4 12.9 %copy-start.10 = (bf16[1,384,768]{2,1,0:T(8,128)(2,1)}, bf16[1,384,768]{2,1,0:T(8,128)(2,1)S(1)}, u32[]{:S(2)}) copy-start(bf16[1,384,768]{2,1,0:T(8,128)(2,1)S(1)} %get-tuple-element.51) | copy-start | bytes 1769476
  315.7 12.6 %copy-start.17 = (f32[768,16]{0,1:T(8,128)}, f32[768,16]{0,1:T(8,128)S(1)}, u32[]{:S(2)}) copy-start(f32[768,16]{0,1:T(8,128)S(1)} %get-tuple-element.44) | copy-start | bytes 147460
  315.7 12.6 %copy-start.18 = (f32[768,16]{0,1:T(8,128)}, f32[768,16]{0,1:T(8,128)S(1)}, u32[]{:S(2)}) copy-start(f32[768,16]{0,1:T(8,128)S(1)} %get-tuple-element.45) | copy-start | bytes 147460
  351.4 40.4 %all-to-all-start.1 = ((bf16[4,32,9216]{2,1,0:T(8,128)(2,1)}), bf16[4,32,9216]{2,1,0:T(8,128)(2,1)}, u32[]{:S(2)}, u32[]{:S(2)}) async-start(bf16[4,32,9216]{2,1,0:T(8,128)(2,1)} %reshape.597), calls=%async_computation.1 | async-start | bytes 4718592 | tf_op jit(solution)/shard_map/all_to_all | solution.py:259
  355.9 12.7 %copy-start.19 = (f32[768,16]{0,1:T(8,128)}, f32[768,16]{0,1:T(8,128)S(1)}, u32[]{:S(2)}) copy-start(f32[768,16]{0,1:T(8,128)S(1)} %get-tuple-element.42) | copy-start | bytes 147460
  355.9 12.7 %copy-start.20 = (f32[768,16]{0,1:T(8,128)}, f32[768,16]{0,1:T(8,128)S(1)}, u32[]{:S(2)}) copy-start(f32[768,16]{0,1:T(8,128)S(1)} %get-tuple-element.43) | copy-start | bytes 147460
  362.3 6.3 copy-start.7
  362.3 6.4 copy-start.11
  391.8 40.5 %all-to-all-start.3 = ((bf16[4,32,9216]{2,1,0:T(8,128)(2,1)}), bf16[4,32,9216]{2,1,0:T(8,128)(2,1)}, u32[]{:S(2)}, u32[]{:S(2)}) async-start(bf16[4,32,9216]{2,1,0:T(8,128)(2,1)} %reshape.600), calls=%async_computation.3 | async-start | bytes 4718592 | tf_op jit(solution)/shard_map/all_to_all | solution.py:259
  396.5 12.7 %copy-start.21 = (f32[768,16]{0,1:T(8,128)}, f32[768,16]{0,1:T(8,128)S(1)}, u32[]{:S(2)}) copy-start(f32[768,16]{0,1:T(8,128)S(1)} %get-tuple-element.40) | copy-start | bytes 147460
  396.5 12.7 %copy-start.22 = (f32[768,16]{0,1:T(8,128)}, f32[768,16]{0,1:T(8,128)S(1)}, u32[]{:S(2)}) copy-start(f32[768,16]{0,1:T(8,128)S(1)} %get-tuple-element.41) | copy-start | bytes 147460
  402.8 6.3 copy-start.8
  402.8 6.4 copy-start.12
  432.3 45.8 %all-to-all-start.5 = ((bf16[4,32,9216]{2,1,0:T(8,128)(2,1)}), bf16[4,32,9216]{2,1,0:T(8,128)(2,1)}, u32[]{:S(2)}, u32[]{:S(2)}) async-start(bf16[4,32,9216]{2,1,0:T(8,128)(2,1)} %reshape.603), calls=%async_computation.5 | async-start | bytes 4718592 | tf_op jit(solution)/shard_map/all_to_all | solution.py:259
  439.7 15.2 %copy-start.23 = (f32[768,16]{0,1:T(8,128)}, f32[768,16]{0,1:T(8,128)S(1)}, u32[]{:S(2)}) copy-start(f32[768,16]{0,1:T(8,128)S(1)} %get-tuple-element.38) | copy-start | bytes 147460
  439.7 15.2 %copy-start.24 = (f32[768,16]{0,1:T(8,128)}, f32[768,16]{0,1:T(8,128)S(1)}, u32[]{:S(2)}) copy-start(f32[768,16]{0,1:T(8,128)S(1)} %get-tuple-element.39) | copy-start | bytes 147460
  448.6 6.4 copy-start.9
  448.6 6.4 copy-start.13
  478.1 4.7 copy-start.16
  478.1 5.4 copy-start.15
  478.1 6.1 copy-start.29
  478.1 32.3 %all-to-all-start.7 = ((bf16[4,32,9216]{2,1,0:T(8,128)(2,1)}), bf16[4,32,9216]{2,1,0:T(8,128)(2,1)S(1)}, u32[]{:S(2)}, u32[]{:S(2)}) async-start(bf16[4,32,9216]{2,1,0:T(8,128)(2,1)} %reshape.606), calls=%async_computation.7 | async-start | bytes 4718592 | tf_op jit(solution)/shard_map/all_to_all | solution.py:259
  518.7 18.7 %copy-start.25 = (bf16[1,1,96,2,96]{2,4,0,3,1:T(8,128)(2,1)S(1)}, bf16[1,1,96,2,96]{2,4,0,3,1:T(8,128)(2,1)}, u32[]{:S(2)}) copy-start(bf16[1,1,96,2,96]{2,4,0,3,1:T(8,128)(2,1)} %get-tuple-element.34) | copy-start | bytes 110596
  518.7 18.7 %copy-start.26 = (bf16[1,1,96,2,96]{2,4,0,3,1:T(8,128)(2,1)S(1)}, bf16[1,1,96,2,96]{2,4,0,3,1:T(8,128)(2,1)}, u32[]{:S(2)}) copy-start(bf16[1,1,96,2,96]{2,4,0,3,1:T(8,128)(2,1)} %get-tuple-element.35) | copy-start | bytes 110596
  537.4 20.2 %copy-start.14 = (f32[256,96]{0,1:T(8,128)S(1)}, f32[256,96]{0,1:T(8,128)}, u32[]{:S(2)}) copy-start(f32[256,96]{0,1:T(8,128)} %convert_element_type.387) | copy-start | bytes 294916
  537.4 20.2 %copy-start.27 = (bf16[1,1,96,2,96]{2,4,0,3,1:T(8,128)(2,1)S(1)}, bf16[1,1,96,2,96]{2,4,0,3,1:T(8,128)(2,1)}, u32[]{:S(2)}) copy-start(bf16[1,1,96,2,96]{2,4,0,3,1:T(8,128)(2,1)} %get-tuple-element.32) | copy-start | bytes 110596
  537.4 20.2 %copy-start.28 = (bf16[1,1,96,2,96]{2,4,0,3,1:T(8,128)(2,1)S(1)}, bf16[1,1,96,2,96]{2,4,0,3,1:T(8,128)(2,1)}, u32[]{:S(2)}) copy-start(bf16[1,1,96,2,96]{2,4,0,3,1:T(8,128)(2,1)} %get-tuple-element.33) | copy-start | bytes 110596
  564.1 4.4 copy-start.37
  573.6 33.1 %all-to-all-start.8 = ((bf16[4,192,1536]{2,1,0:T(8,128)(2,1)}), bf16[4,192,1536]{2,1,0:T(8,128)(2,1)}, u32[]{:S(2)}, u32[]{:S(2)}) async-start(bf16[4,192,1536]{2,1,0:T(8,128)(2,1)} %reshape.610), calls=%async_computation.8 | async-start | bytes 4718592 | tf_op jit(solution)/shard_map/all_to_all | solution.py:286
  606.7 33.1 %all-to-all-start.11 = ((bf16[4,192,1536]{2,1,0:T(8,128)(2,1)}), bf16[4,192,1536]{2,1,0:T(8,128)(2,1)}, u32[]{:S(2)}, u32[]{:S(2)}) async-start(bf16[4,192,1536]{2,1,0:T(8,128)(2,1)} %reshape.614), calls=%async_computation.11 | async-start | bytes 4718592 | tf_op jit(solution)/shard_map/all_to_all | solution.py:286
  639.8 33.2 %all-to-all-start.14 = ((bf16[4,192,1536]{2,1,0:T(8,128)(2,1)}), bf16[4,192,1536]{2,1,0:T(8,128)(2,1)}, u32[]{:S(2)}, u32[]{:S(2)}) async-start(bf16[4,192,1536]{2,1,0:T(8,128)(2,1)} %reshape.618), calls=%async_computation.14 | async-start | bytes 4718592 | tf_op jit(solution)/shard_map/all_to_all | solution.py:286
  673.1 32.1 %all-to-all-start.17 = ((bf16[4,192,1536]{2,1,0:T(8,128)(2,1)}), bf16[4,192,1536]{2,1,0:T(8,128)(2,1)S(1)}, u32[]{:S(2)}, u32[]{:S(2)}) async-start(bf16[4,192,1536]{2,1,0:T(8,128)(2,1)} %reshape.622), calls=%async_computation.17 | async-start | bytes 4718592 | tf_op jit(solution)/shard_map/all_to_all | solution.py:286
  705.2 1.4 copy-start.5
  706.6 56.5 %all-to-all-start.9 = ((bf16[8,192,768]{2,1,0:T(8,128)(2,1)}), bf16[8,192,768]{2,1,0:T(8,128)(2,1)S(1)}, u32[]{:S(2)}, u32[]{:S(2)}) async-start(bf16[8,192,768]{2,1,0:T(8,128)(2,1)} %bitcast.472), calls=%async_computation.9 | async-start | bytes 4718592 | tf_op jit(solution)/shard_map/all_to_all | solution.py:298
  712.9 184.3 %all-gather.5.cloned.1.call-start = ((), (), s32[]{:S(2)}) async-start(), calls=%async_computation.20 | async-start | bytes 7077888 | tf_op jit(solution)/shard_map/all_gather | solution.py:205
  763.1 1.4 copy-start.2
  764.5 57.4 %all-to-all-start.12 = ((bf16[8,192,768]{2,1,0:T(8,128)(2,1)}), bf16[8,192,768]{2,1,0:T(8,128)(2,1)S(1)}, u32[]{:S(2)}, u32[]{:S(2)}) async-start(bf16[8,192,768]{2,1,0:T(8,128)(2,1)} %bitcast.473), calls=%async_computation.12 | async-start | bytes 4718592 | tf_op jit(solution)/shard_map/all_to_all | solution.py:298
  786.4 44.8 %copy-start.31 = (f32[1536]{0:T(1024)S(1)}, f32[1536]{0:T(1024)}, u32[]{:S(2)}) copy-start(f32[1536]{0:T(1024)} %param.25) | copy-start | bytes 18436
  786.4 44.8 %copy-start.32 = (f32[384]{0:T(512)S(1)}, f32[384]{0:T(512)}, u32[]{:S(2)}) copy-start(f32[384]{0:T(512)} %param.27) | copy-start | bytes 4612
  821.9 56.9 %all-to-all-start.15 = ((bf16[8,192,768]{2,1,0:T(8,128)(2,1)}), bf16[8,192,768]{2,1,0:T(8,128)(2,1)}, u32[]{:S(2)}, u32[]{:S(2)}) async-start(bf16[8,192,768]{2,1,0:T(8,128)(2,1)} %bitcast.471), calls=%async_computation.15 | async-start | bytes 4718592 | tf_op jit(solution)/shard_map/all_to_all | solution.py:298
  830.5 105.6 %all-gather.7.cloned.1.call-start = ((), (), s32[]{:S(2)}) async-start(), calls=%async_computation.21 | async-start | bytes 7077888 | tf_op jit(solution)/shard_map/all_gather | solution.py:206
  847.0 7.8 copy-start.3
  878.8 137.4 %all-to-all-start.18 = ((bf16[8,192,768]{2,1,0:T(8,128)(2,1)}), bf16[8,192,768]{2,1,0:T(8,128)(2,1)}, u32[]{:S(2)}, u32[]{:S(2)}) async-start(bf16[8,192,768]{2,1,0:T(8,128)(2,1)} %bitcast.470), calls=%async_computation.18 | async-start | bytes 4718592 | tf_op jit(solution)/shard_map/all_to_all | solution.py:298
  892.8 43.3 %copy-start.30 = (f32[3072]{0:T(1024)S(1)}, f32[3072]{0:T(1024)}, u32[]{:S(2)}) copy-start(f32[3072]{0:T(1024)} %add.367) | copy-start | bytes 36868
  892.8 43.3 %copy-start.33 = (f32[768]{0:T(1024)S(1)}, f32[768]{0:T(1024)}, u32[]{:S(2)}) copy-start(f32[768]{0:T(1024)} %param.23) | copy-start | bytes 9220
  892.8 43.3 %copy-start.34 = (f32[768]{0:T(1024)S(1)}, f32[768]{0:T(1024)}, u32[]{:S(2)}) copy-start(f32[768]{0:T(1024)} %param.22) | copy-start | bytes 9220
  965.9 4.2 copy-start.4
  1016.2 46.4 %all-to-all-start.10 = ((bf16[2,1536,384]{2,1,0:T(8,128)(2,1)}), bf16[2,1536,384]{2,1,0:T(8,128)(2,1)S(1)}, u32[]{:S(2)}, u32[]{:S(2)}) async-start(bf16[2,1536,384]{2,1,0:T(8,128)(2,1)} %bitcast.466), calls=%async_computation.10 | async-start | bytes 4718592 | tf_op jit(solution)/shard_map/all_to_all | solution.py:315
  1062.6 33.1 %all-to-all-start.13 = ((bf16[2,1536,384]{2,1,0:T(8,128)(2,1)}), bf16[2,1536,384]{2,1,0:T(8,128)(2,1)}, u32[]{:S(2)}, u32[]{:S(2)}) async-start(bf16[2,1536,384]{2,1,0:T(8,128)(2,1)} %bitcast.468), calls=%async_computation.13 | async-start | bytes 4718592 | tf_op jit(solution)/shard_map/all_to_all | solution.py:315
  1095.7 38.2 %all-to-all-start.16 = ((bf16[2,1536,384]{2,1,0:T(8,128)(2,1)}), bf16[2,1536,384]{2,1,0:T(8,128)(2,1)}, u32[]{:S(2)}, u32[]{:S(2)}) async-start(bf16[2,1536,384]{2,1,0:T(8,128)(2,1)} %bitcast.467), calls=%async_computation.16 | async-start | bytes 4718592 | tf_op jit(solution)/shard_map/all_to_all | solution.py:315
  1172.3 8.7 copy-start.1
Sparse Core Ops, SparseCore 0:
  715.3 101.8 all-gather.4
  832.8 103.1 all-gather.6
